TPU v7x, 32 devices: a whole 2x2x4 slice. The times are simulated.
32 devices in a mesh: pulse: 4 (over z), range: 4 (over y, core), tile: 2 (over x).
Axes of the slice: x: 2, y: 2, z: 4, core: 2. Of those that a mesh axis runs over, the one named last changes fastest.
Arguments:
- echo: bfloat16 [2, 64, 32768], P(None, ('pulse', 'tile'), 'range'), may hold values from -6 to 6
- replica: bfloat16 [2, 4096], replicated, may hold values from -0.09375 to 0.09375
- interp: bfloat16 [32, 256, 128], P('range'), may hold values from -0.375 to 0.375
- band_start: int32 [64, 2, 4], P(('pulse', 'tile'), None, 'range'), may hold values from 0 to 7040, as said below
- visible: int32 [64, 2], P(('pulse', 'tile')), may hold values 0 or 1
- doppler: int32 [64], P(('pulse', 'tile')), may hold values from 0 to 511
- range_step: int32 [64], P(('pulse', 'tile')), may hold values from 0 to 4095
Outputs:
- image: float32 [2, 512, 4096], P(None, ('tile', 'pulse'), 'range')
Inputs may be any that keep to these rules, and one draw needn't show every extreme that they name: band_start is counted within the 8192 bins of range block b and is a multiple of 128; the values 0 and 7040 both occur.
All inputs are finite; a program needn't handle non-finite values. No bound on the sum of `visible` on one device may be relied on, other than what follows from the above.
Results may differ from a plain program's by a relative error of at most 0.0047.
Values may be sent and summed in bfloat16 or wider, within the bound.
A program may use at most 64 MiB of HBM per device.

v0:
```python
import functools
import math

import jax
import jax.numpy as jnp
from jax import lax
from jax.experimental import pallas as pl
from jax.experimental.pallas import tpu as pltpu
from jax.sharding import PartitionSpec as P

AZ_DEV = 64
LANES = 128
TILE_GROUP = 2
MESH = pl.DeviceIdType.MESH


def each(count, body):
    if count <= 16:
        for step in range(count):
            body(step)
    else:
        lax.fori_loop(0, count, lambda step, carry: (body(step), carry)[1], 0)


def wrap(value, total):
    if total & (total - 1) == 0:
        return value & (total - 1)
    return lax.rem(value, jnp.int32(total))


def image_kernel(
    sizes,
    starts_in, visible_in, doppler_in, step_in,
    echo_in, replica_in, interp_in,
    all_rows, factor_ref,
    starts_ref, visible_ref, doppler_ref, step_ref,
    echo_ref, replica_ref, interp_ref, load_sem,
    left_halo, right_halo, ext_re, ext_im, gat_re, gat_im, gat, chirp,
    turn_cos, turn_sin, own_bins, all_bins, own_rows, own_sem,
    halo_send, halo_recv, bins_send, bins_recv, rows_send, rows_recv,
):
    pulses, tiles, groups, ranges, band_blocks, chirp_blocks, samp_blocks, lines = sizes
    half_blocks = chirp_blocks // 2
    half = half_blocks * LANES
    samples = samp_blocks * LANES
    members = groups * tiles
    seen_blocks = band_blocks + chirp_blocks
    seen_pad = gat_re.shape[0] // (TILE_GROUP * pulses)
    group_id = lax.axis_index("pulse")
    tile_id = lax.axis_index("tile")
    range_id = lax.axis_index("range")
    me = group_id * tiles + tile_id

    def member(offset):
        other = lax.rem(me + offset, members)
        return other, {"pulse": other // tiles, "tile": lax.rem(other, tiles)}

    places = (
        (step_in, step_ref), (doppler_in, doppler_ref), (visible_in, visible_ref), (starts_in, starts_ref),
        (replica_in, replica_ref), (echo_in, echo_ref), (interp_in, interp_ref),
    )
    loads = [
        pltpu.make_async_copy(there, here, load_sem.at[place]) for place, (there, here) in enumerate(places)
    ]
    load_step, load_doppler, load_visible, load_starts, load_replica, load_echo, load_interp = loads
    for load in loads:
        load.start()

    barrier = pltpu.get_barrier_semaphore()

    @pl.when(range_id > 0)
    def _():
        pl.semaphore_signal(barrier, inc=1, device_id={"range": range_id - 1}, device_id_type=MESH)

    @pl.when(range_id < ranges - 1)
    def _():
        pl.semaphore_signal(barrier, inc=1, device_id={"range": range_id + 1}, device_id_type=MESH)

    def greet(step):
        _, where = member(step + 1)
        pl.semaphore_signal(barrier, inc=1, device_id=where, device_id_type=MESH)

    each(members - 1, greet)
    load_step.wait()
    line_number = range_id * lines + lax.broadcasted_iota(jnp.int32, (pulses, lines), 1)
    pulse_row = lax.broadcasted_iota(jnp.int32, (pulses, lines), 0)
    steps = jnp.zeros((pulses, lines), jnp.int32)
    for q in range(pulses):
        steps = jnp.where(pulse_row == q, step_ref[q], steps)
    range_total = lines * ranges
    angle = wrap(steps * line_number, range_total).astype(jnp.float32) * (2.0 * math.pi / range_total)
    turn_cos[...] = jnp.cos(angle)
    turn_sin[...] = jnp.sin(angle)

    neighbours = (range_id > 0).astype(jnp.int32) + (range_id < ranges - 1).astype(jnp.int32)
    pl.semaphore_wait(barrier, members - 1 + neighbours)

    to_left = pltpu.make_async_remote_copy(
        src_ref=echo_in.at[:, pl.ds(0, half)], dst_ref=right_halo,
        send_sem=halo_send.at[0], recv_sem=halo_recv.at[0],
        device_id={"range": lax.max(range_id - 1, 0)}, device_id_type=MESH,
    )
    to_right = pltpu.make_async_remote_copy(
        src_ref=echo_in.at[:, pl.ds(samples - half, half)], dst_ref=left_halo,
        send_sem=halo_send.at[1], recv_sem=halo_recv.at[1],
        device_id={"range": lax.min(range_id + 1, ranges - 1)}, device_id_type=MESH,
    )

    @pl.when(range_id > 0)
    def _():
        to_left.start()

    @pl.when(range_id < ranges - 1)
    def _():
        to_right.start()

    load_doppler.wait()
    load_visible.wait()
    load_starts.wait()
    lane = lax.broadcasted_iota(jnp.int32, (8, LANES), 1)
    row = lax.broadcasted_iota(jnp.int32, (8, LANES), 0)
    lane_pulse = lane % pulses
    bins = jnp.zeros((8, LANES), jnp.int32)
    for q in range(pulses):
        bins = jnp.where(lane_pulse == q, doppler_ref[q], bins)

    def fill_bins(tile):
        flags = jnp.zeros((8, LANES), jnp.int32)
        for q in range(pulses):
            flags = jnp.where(lane_pulse == q, visible_ref[tile, q], flags)
        own_bins[tile] = jnp.where(row == 0, bins, flags)

    each(tiles, fill_bins)

    def bins_copy(step):
        other, where = member(step + 1)
        return pltpu.make_async_remote_copy(
            src_ref=own_bins.at[lax.rem(other, tiles)], dst_ref=all_bins.at[me],
            send_sem=bins_send.at[step], recv_sem=bins_recv.at[step],
            device_id=where, device_id_type=MESH,
        )

    each(members - 1, lambda step: bins_copy(step).start())
    all_bins[me] = own_bins[tile_id]

    load_replica.wait()

    wide = (chirp_blocks + 1) * LANES

    def shifted(part):
        taps = replica_ref[...].astype(jnp.float32)[part:part + 1, :]
        taps = jnp.concatenate([taps, jnp.zeros((1, LANES), jnp.float32)], axis=1)
        spread = jnp.broadcast_to(taps, (LANES, wide))
        return pltpu.roll(spread, 0, 1, stride=1, stride_axis=0).astype(jnp.bfloat16)

    shifted_re = shifted(0)
    for turn in range(chirp_blocks + 1):
        block = shifted_re[:, turn * LANES:(turn + 1) * LANES]
        chirp[turn, :LANES, :LANES] = block
        chirp[turn, LANES:, LANES:] = block
    shifted_im = shifted(1)
    for turn in range(chirp_blocks + 1):
        block = shifted_im[:, turn * LANES:(turn + 1) * LANES]
        chirp[turn, :LANES, LANES:] = block
        chirp[turn, LANES:, :LANES] = -block

    def lay(block, values):
        ext_re[block * pulses:(block + 1) * pulses, :] = values[:pulses]
        ext_im[block * pulses:(block + 1) * pulses, :] = values[pulses:]

    load_echo.wait()
    for block in range(samp_blocks):
        lay(half_blocks + block, echo_ref[:, block * LANES:(block + 1) * LANES].astype(jnp.float32))
    filled = samp_blocks + 2 * half_blocks
    tail = ext_re.shape[0] - filled * pulses
    ext_re[filled * pulses:, :] = jnp.zeros((tail, LANES), jnp.float32)
    ext_im[filled * pulses:, :] = jnp.zeros((tail, LANES), jnp.float32)

    @pl.when(range_id > 0)
    def _():
        to_right.wait_recv()

    @pl.when(range_id == 0)
    def _():
        left_halo[...] = jnp.zeros_like(left_halo)

    @pl.when(range_id < ranges - 1)
    def _():
        to_left.wait_recv()

    @pl.when(range_id == ranges - 1)
    def _():
        right_halo[...] = jnp.zeros_like(right_halo)

    for block in range(half_blocks):
        lay(block, left_halo[:, block * LANES:(block + 1) * LANES].astype(jnp.float32))
        lay(
            half_blocks + samp_blocks + block,
            right_halo[:, block * LANES:(block + 1) * LANES].astype(jnp.float32),
        )

    load_interp.wait()

    rows = TILE_GROUP * pulses

    def tile_pair(pair):
        for which in range(TILE_GROUP):
            for q in range(pulses):
                first = starts_ref[pair * TILE_GROUP + which, 0, q] // LANES
                source = pl.ds(first * pulses + q, seen_pad, stride=pulses)
                target = pl.ds(which * pulses + q, seen_pad, stride=rows)
                gat_re[target, :] = ext_re[source, :]
                gat_im[target, :] = ext_im[source, :]
        gat[:, :LANES] = gat_re[...].astype(jnp.bfloat16)
        gat[:, LANES:] = gat_im[...].astype(jnp.bfloat16)
        total = jnp.zeros((band_blocks * rows, 2 * LANES), jnp.float32)
        for turn in range(chirp_blocks + 1):
            total = total + lax.dot_general(
                gat[turn * rows:(turn + band_blocks) * rows, :], chirp[turn],
                (((1,), (1,)), ((), ())), preferred_element_type=jnp.float32,
            )
        bands = total.astype(jnp.bfloat16)
        for j in range(band_blocks - 1):
            here = bands[j * rows:(j + 1) * rows]
            after = bands[(j + 1) * rows:(j + 2) * rows]
            window = jnp.concatenate(
                [
                    jnp.concatenate([here[:, :LANES], after[:, :LANES]], axis=1),
                    jnp.concatenate([here[:, LANES:], after[:, LANES:]], axis=1),
                ],
                axis=0,
            )
            values = jnp.dot(window, interp_ref[j], preferred_element_type=jnp.float32)
            cosine = turn_cos[:, j * LANES:(j + 1) * LANES]
            sine = turn_sin[:, j * LANES:(j + 1) * LANES]
            for which in range(TILE_GROUP):
                real = values[which * pulses:(which + 1) * pulses]
                imag = values[rows + which * pulses:rows + (which + 1) * pulses]
                steered = jnp.concatenate(
                    [real * cosine - imag * sine, real * sine + imag * cosine], axis=0
                )
                own_rows[pair * TILE_GROUP + which, :, j * LANES:(j + 1) * LANES] = steered.astype(jnp.bfloat16)

    each(tiles // TILE_GROUP, tile_pair)

    def rows_copy(step):
        other, where = member(step + 1)
        return pltpu.make_async_remote_copy(
            src_ref=own_rows.at[lax.rem(other, tiles)], dst_ref=all_rows.at[me],
            send_sem=rows_send.at[step], recv_sem=rows_recv.at[step],
            device_id=where, device_id_type=MESH,
        )

    each(members - 1, lambda step: rows_copy(step).start())
    keep_own = pltpu.make_async_copy(own_rows.at[tile_id], all_rows.at[me], own_sem)
    keep_own.start()

    each(members - 1, lambda step: bins_copy(step).wait_recv())
    azimuth_total = AZ_DEV * members
    norm_scale = (pulses * members) ** (-0.5)
    per_member = 2 * pulses
    per_chunk = LANES // per_member
    first_line = tile_id * (groups * AZ_DEV) + group_id * AZ_DEV
    az_line = first_line + lax.broadcasted_iota(jnp.int32, (AZ_DEV, LANES), 0)
    az_lane = lax.broadcasted_iota(jnp.int32, (AZ_DEV, LANES), 1)
    is_imag = (az_lane // pulses) % 2 == 1
    for chunk in range(members // per_chunk):
        known = jnp.zeros((8, LANES), jnp.int32)
        for at in range(per_chunk):
            known = jnp.where(lane // per_member == at, all_bins[chunk * per_chunk + at], known)
        angle = wrap(az_line * known[0:1, :], azimuth_total).astype(jnp.float32) * (2.0 * math.pi / azimuth_total)
        weight = known[1:2, :].astype(jnp.float32) * norm_scale
        factor_re = jnp.cos(angle) * weight
        factor_im = jnp.sin(angle) * weight
        factor_ref[:, chunk * LANES:(chunk + 1) * LANES] = jnp.concatenate(
            [jnp.where(is_imag, -factor_im, factor_re), jnp.where(is_imag, factor_re, factor_im)], axis=0
        ).astype(jnp.bfloat16)

    each(members - 1, lambda step: rows_copy(step).wait_recv())
    keep_own.wait()

    @pl.when(range_id > 0)
    def _():
        to_left.wait_send()

    @pl.when(range_id < ranges - 1)
    def _():
        to_right.wait_send()

    each(members - 1, lambda step: bins_copy(step).wait_send())
    each(members - 1, lambda step: rows_copy(step).wait_send())


def local(echo, replica, interp, band_start, visible, doppler, range_step):
    chirp_blocks = replica.shape[1] // LANES
    pulses = echo.shape[1]
    samples = echo.shape[2]
    samp_blocks = samples // LANES
    lines = interp.shape[0] * interp.shape[2]
    band_blocks = interp.shape[0] + 1
    tiles = lax.axis_size("tile")
    groups = lax.axis_size("pulse")
    ranges = lax.axis_size("range")
    members = tiles * groups
    half = chirp_blocks * LANES // 2
    rows = TILE_GROUP * pulses
    seen_pad = -(-(band_blocks + chirp_blocks) // 8) * 8
    ext_blocks = samp_blocks + chirp_blocks + 8
    sizes = (pulses, tiles, groups, ranges, band_blocks, chirp_blocks, samp_blocks, lines)
    hbm = pl.BlockSpec(memory_space=pl.ANY)
    vmem = pl.BlockSpec(memory_space=pltpu.VMEM)
    rows_out, factors = pl.pallas_call(
        functools.partial(image_kernel, sizes),
        out_shape=(
            jax.ShapeDtypeStruct((members, 2 * pulses, lines), jnp.bfloat16),
            jax.ShapeDtypeStruct((2 * AZ_DEV, members * 2 * pulses), jnp.bfloat16),
        ),
        in_specs=[hbm] * 7,
        out_specs=(hbm, vmem),
        scratch_shapes=[
            pltpu.SMEM((tiles, 1, pulses), jnp.int32),
            pltpu.SMEM((tiles, pulses), jnp.int32),
            pltpu.SMEM((pulses,), jnp.int32),
            pltpu.SMEM((pulses,), jnp.int32),
            pltpu.VMEM((2 * pulses, samples), jnp.bfloat16),
            pltpu.VMEM(replica.shape, jnp.bfloat16),
            pltpu.VMEM(interp.shape, jnp.bfloat16),
            pltpu.SemaphoreType.DMA((7,)),
            pltpu.VMEM((2 * pulses, half), jnp.bfloat16),
            pltpu.VMEM((2 * pulses, half), jnp.bfloat16),
            pltpu.VMEM((ext_blocks * pulses, LANES), jnp.float32),
            pltpu.VMEM((ext_blocks * pulses, LANES), jnp.float32),
            pltpu.VMEM((seen_pad * rows, LANES), jnp.float32),
            pltpu.VMEM((seen_pad * rows, LANES), jnp.float32),
            pltpu.VMEM((seen_pad * rows, 2 * LANES), jnp.bfloat16),
            pltpu.VMEM((chirp_blocks + 1, 2 * LANES, 2 * LANES), jnp.bfloat16),
            pltpu.VMEM((pulses, lines), jnp.float32),
            pltpu.VMEM((pulses, lines), jnp.float32),
            pltpu.VMEM((tiles, 8, LANES), jnp.int32),
            pltpu.VMEM((members, 8, LANES), jnp.int32),
            pltpu.VMEM((tiles, 2 * pulses, lines), jnp.bfloat16),
            pltpu.SemaphoreType.DMA,
            pltpu.SemaphoreType.DMA((2,)),
            pltpu.SemaphoreType.DMA((2,)),
            pltpu.SemaphoreType.DMA((members - 1,)),
            pltpu.SemaphoreType.DMA((members - 1,)),
            pltpu.SemaphoreType.DMA((members - 1,)),
            pltpu.SemaphoreType.DMA((members - 1,)),
        ],
        compiler_params=pltpu.CompilerParams(
            collective_id=0, has_side_effects=True, vmem_limit_bytes=60 * 1024 * 1024
        ),
        name="backproject",
    )(
        band_start.transpose(1, 2, 0), visible.T, doppler, range_step,
        echo.reshape(2 * pulses, samples), replica, interp,
    )
    image = jnp.dot(
        factors, rows_out.reshape(members * 2 * pulses, lines), preferred_element_type=jnp.float32
    )
    return image.reshape(2, AZ_DEV, lines)


def solution(mesh):
    in_specs = (
        P(None, ("pulse", "tile"), "range"),
        P(),
        P("range", None, None),
        P(("pulse", "tile"), None, "range"),
        P(("pulse", "tile"), None),
        P(("pulse", "tile")),
        P(("pulse", "tile")),
    )
    out_specs = P(None, ("tile", "pulse"), "range")
    return jax.shard_map(local, mesh=mesh, in_specs=in_specs, out_specs=out_specs, check_vma=False)
```

profile of v0, /device:TPU:1, one launch (start us, length us, event | category | flops | bytes accessed | tf_op | source)
XLA Modules:
  0.0 18.1 jit_solution(9103904194094493710)
XLA Ops:
  0.0 16.1 %backproject.1 = (bf16[8,16,1024]{2,1,0:T(8,128)(2,1)}, bf16[128,128]{1,0:T(8,128)(2,1)}) custom-call(s32[2,1,8]{2,1,0:T(1,128)} %bitcast.12, s32[2,8]{1,0:T(2,128)} %bitcast.13, s32[8]{0:T(128)} %doppler_in.1, s32[8]{0:T(128)} %step_in.1, bf16[16,8192]{1,0:T(8,128)(2,1)} %bitcast.10, bf16[2,4096]{1,0:T(2,128)(2,1)} %replica_in.1, bf16[8,256,128]{2,1,0:T(8,128)(2,1)} %interp_in.1), custom_call_target="tpu_custom_call" | custom-call | tf_op jit(solution)/shard_map/backproject/pallas_call | solution.py:312
  16.2 2.0 %fusion = f32[2,64,1024]{2,1,0:T(8,128)} fusion(bf16[2,64,128]{2,1,0:T(8,128)(2,1)} %bitcast.11, bf16[128,1024,1]{1,0,2:T(8,128)(2,1)} %bitcast.9), kind=kOutput, calls=%fused_computation | convolution fusion | flops 33554432 | bytes 819200 | tf_op jit(solution)/shard_map/dot_general | solution.py:358
where the time goes:
time: 18.3 us; the launch traced here: 18.1 us
  Pallas kernels  16.1 us (88%)
  matrix products  1.98 us (11%)
    pallas_call x1, Pallas kernels, local(): pl.pallas_call(functools.partial(image_kernel, sizes), out_shape=(jax.Sha...  16.1 us
    dot_general x1, matrix products, local(): jnp.dot(factors, rows_out.reshape(members * 2 * pulses, lines), preferred...  1.98 us

commit v1 on v0

--- a/solution.py
+++ b/solution.py
@@ -14,12 +14,12 @@
 MESH = pl.DeviceIdType.MESH
 
 
-def each(count, body):
+def each(count, body, first=0):
     if count <= 16:
-        for step in range(count):
+        for step in range(first, count):
             body(step)
     else:
-        lax.fori_loop(0, count, lambda step, carry: (body(step), carry)[1], 0)
+        lax.fori_loop(first, count, lambda step, carry: (body(step), carry)[1], 0)
 
 
 def wrap(value, total):
@@ -37,7 +37,7 @@
     echo_ref, replica_ref, interp_ref, load_sem,
     left_halo, right_halo, ext_re, ext_im, gat_re, gat_im, gat, chirp,
     turn_cos, turn_sin, own_bins, all_bins, own_rows, own_sem,
-    halo_send, halo_recv, bins_send, bins_recv, rows_send, rows_recv,
+    halo_send, halo_recv, bins_send, bins_recv, rows_send, rows_recv, relay_send,
 ):
     pulses, tiles, groups, ranges, band_blocks, chirp_blocks, samp_blocks, lines = sizes
     half_blocks = chirp_blocks // 2
@@ -51,9 +51,16 @@
     range_id = lax.axis_index("range")
     me = group_id * tiles + tile_id
 
-    def member(offset):
-        other = lax.rem(me + offset, members)
-        return other, {"pulse": other // tiles, "tile": lax.rem(other, tiles)}
+    turns = [2 % groups] + [turn for turn in range(1, groups) if turn != 2 % groups] + [0]
+
+    def others(body, which=None):
+        for turn in turns if which is None else which:
+            each(tiles, functools.partial(body, turn), first=1 if turn == 0 else 0)
+
+    def member(turn, step):
+        group = lax.rem(group_id + turn, groups)
+        tile = lax.rem(tile_id + step, tiles)
+        return tile, {"pulse": group, "tile": tile}
 
     places = (
         (step_in, step_ref), (doppler_in, doppler_ref), (visible_in, visible_ref), (starts_in, starts_ref),
@@ -76,11 +83,11 @@
     def _():
         pl.semaphore_signal(barrier, inc=1, device_id={"range": range_id + 1}, device_id_type=MESH)
 
-    def greet(step):
-        _, where = member(step + 1)
+    def greet(turn, step):
+        _, where = member(turn, step)
         pl.semaphore_signal(barrier, inc=1, device_id=where, device_id_type=MESH)
 
-    each(members - 1, greet)
+    others(greet)
     load_step.wait()
     line_number = range_id * lines + lax.broadcasted_iota(jnp.int32, (pulses, lines), 1)
     pulse_row = lax.broadcasted_iota(jnp.int32, (pulses, lines), 0)
@@ -132,15 +139,15 @@
 
     each(tiles, fill_bins)
 
-    def bins_copy(step):
-        other, where = member(step + 1)
+    def bins_copy(turn, step):
+        tile, where = member(turn, step)
         return pltpu.make_async_remote_copy(
-            src_ref=own_bins.at[lax.rem(other, tiles)], dst_ref=all_bins.at[me],
-            send_sem=bins_send.at[step], recv_sem=bins_recv.at[step],
+            src_ref=own_bins.at[tile], dst_ref=all_bins.at[me],
+            send_sem=bins_send.at[turn * tiles + step], recv_sem=bins_recv.at[turn * tiles + step],
             device_id=where, device_id_type=MESH,
         )
 
-    each(members - 1, lambda step: bins_copy(step).start())
+    others(lambda turn, step: bins_copy(turn, step).start())
     all_bins[me] = own_bins[tile_id]
 
     load_replica.wait()
@@ -202,8 +209,13 @@
     load_interp.wait()
 
     rows = TILE_GROUP * pulses
-
-    def tile_pair(pair):
+    cut = band_blocks // 2 + 1
+    parts = [(0, cut), (cut, band_blocks)] if tiles == TILE_GROUP else [(0, band_blocks)]
+    spans = [
+        pl.ds(max(start - 1, 0) * LANES, (stop - 1 - max(start - 1, 0)) * LANES) for start, stop in parts
+    ]
+
+    def gather(pair):
         for which in range(TILE_GROUP):
             for q in range(pulses):
                 first = starts_ref[pair * TILE_GROUP + which, 0, q] // LANES
@@ -213,16 +225,17 @@
                 gat_im[target, :] = ext_im[source, :]
         gat[:, :LANES] = gat_re[...].astype(jnp.bfloat16)
         gat[:, LANES:] = gat_im[...].astype(jnp.bfloat16)
-        total = jnp.zeros((band_blocks * rows, 2 * LANES), jnp.float32)
+
+    def steer(pair, start, stop, before):
+        total = jnp.zeros(((stop - start) * rows, 2 * LANES), jnp.float32)
         for turn in range(chirp_blocks + 1):
             total = total + lax.dot_general(
-                gat[turn * rows:(turn + band_blocks) * rows, :], chirp[turn],
+                gat[(turn + start) * rows:(turn + stop) * rows, :], chirp[turn],
                 (((1,), (1,)), ((), ())), preferred_element_type=jnp.float32,
             )
-        bands = total.astype(jnp.bfloat16)
-        for j in range(band_blocks - 1):
-            here = bands[j * rows:(j + 1) * rows]
-            after = bands[(j + 1) * rows:(j + 2) * rows]
+        made = total.astype(jnp.bfloat16)
+        bands = before + [made[j * rows:(j + 1) * rows] for j in range(stop - start)]
+        for here, after, j in zip(bands, bands[1:], range(start - len(before), stop - 1)):
             window = jnp.concatenate(
                 [
                     jnp.concatenate([here[:, :LANES], after[:, :LANES]], axis=1),
@@ -240,22 +253,52 @@
                     [real * cosine - imag * sine, real * sine + imag * cosine], axis=0
                 )
                 own_rows[pair * TILE_GROUP + which, :, j * LANES:(j + 1) * LANES] = steered.astype(jnp.bfloat16)
-
-    each(tiles // TILE_GROUP, tile_pair)
-
-    def rows_copy(step):
-        other, where = member(step + 1)
+        return bands[-1:]
+
+    relay = groups == 4
+    relays = jnp.logical_or(group_id == 1, group_id == groups - 2)
+
+    def rows_copy(part, turn, step):
+        tile, where = member(turn, step)
         return pltpu.make_async_remote_copy(
-            src_ref=own_rows.at[lax.rem(other, tiles)], dst_ref=all_rows.at[me],
-            send_sem=rows_send.at[step], recv_sem=rows_recv.at[step],
+            src_ref=own_rows.at[tile, :, spans[part]], dst_ref=all_rows.at[me, :, spans[part]],
+            send_sem=rows_send.at[part, turn * tiles + step], recv_sem=rows_recv.at[part, turn * tiles + step],
             device_id=where, device_id_type=MESH,
         )
 
-    each(members - 1, lambda step: rows_copy(step).start())
+    def when_direct(act):
+        def body(turn, step):
+            if relay and turn in (1, groups - 1):
+                pl.when(group_id != (groups - 1 if turn == 1 else 0))(lambda: act(turn, step))
+            else:
+                act(turn, step)
+
+        others(body)
+
+    def relay_copy(part, step):
+        far = jnp.where(group_id == 1, groups - 1, 0)
+        slot = far * tiles + lax.rem(tile_id - step + tiles, tiles)
+        end = jnp.where(group_id == 1, 0, groups - 1)
+        arrival = jnp.where(group_id == 1, 1, groups - 1) * tiles + step
+        return pltpu.make_async_remote_copy(
+            src_ref=all_rows.at[slot, :, spans[part]], dst_ref=all_rows.at[slot, :, spans[part]],
+            send_sem=relay_send.at[part, step], recv_sem=rows_recv.at[part, arrival],
+            device_id={"pulse": end, "tile": tile_id}, device_id_type=MESH,
+        )
+
+    last = []
+    for part, (start, stop) in enumerate(parts):
+        if tiles == TILE_GROUP:
+            if part == 0:
+                gather(0)
+            last = steer(0, start, stop, last)
+        else:
+            each(tiles // TILE_GROUP, lambda pair: (gather(pair), steer(pair, start, stop, [])))
+        when_direct(lambda turn, step: rows_copy(part, turn, step).start())
     keep_own = pltpu.make_async_copy(own_rows.at[tile_id], all_rows.at[me], own_sem)
     keep_own.start()
 
-    each(members - 1, lambda step: bins_copy(step).wait_recv())
+    others(lambda turn, step: bins_copy(turn, step).wait_recv())
     azimuth_total = AZ_DEV * members
     norm_scale = (pulses * members) ** (-0.5)
     per_member = 2 * pulses
@@ -276,7 +319,17 @@
             [jnp.where(is_imag, -factor_im, factor_re), jnp.where(is_imag, factor_re, factor_im)], axis=0
         ).astype(jnp.bfloat16)
 
-    each(members - 1, lambda step: rows_copy(step).wait_recv())
+    if relay:
+        for part in range(len(parts)):
+            others(lambda turn, step: rows_copy(part, turn, step).wait_recv(), [2])
+
+            @pl.when(relays)
+            def _():
+                each(tiles, lambda step: relay_copy(part, step).start())
+
+    for part in range(len(parts)):
+        rest = [turn for turn in turns if not (relay and turn == 2)]
+        others(lambda turn, step: rows_copy(part, turn, step).wait_recv(), rest)
     keep_own.wait()
 
     @pl.when(range_id > 0)
@@ -287,8 +340,15 @@
     def _():
         to_right.wait_send()
 
-    each(members - 1, lambda step: bins_copy(step).wait_send())
-    each(members - 1, lambda step: rows_copy(step).wait_send())
+    others(lambda turn, step: bins_copy(turn, step).wait_send())
+    for part in range(len(parts)):
+        when_direct(lambda turn, step: rows_copy(part, turn, step).wait_send())
+    if relay:
+
+        @pl.when(relays)
+        def _():
+            for part in range(len(parts)):
+                each(tiles, lambda step: relay_copy(part, step).wait_send())
 
 
 def local(echo, replica, interp, band_start, visible, doppler, range_step):
@@ -342,10 +402,11 @@
             pltpu.SemaphoreType.DMA,
             pltpu.SemaphoreType.DMA((2,)),
             pltpu.SemaphoreType.DMA((2,)),
-            pltpu.SemaphoreType.DMA((members - 1,)),
-            pltpu.SemaphoreType.DMA((members - 1,)),
-            pltpu.SemaphoreType.DMA((members - 1,)),
-            pltpu.SemaphoreType.DMA((members - 1,)),
+            pltpu.SemaphoreType.DMA((members,)),
+            pltpu.SemaphoreType.DMA((members,)),
+            pltpu.SemaphoreType.DMA((2, members)),
+            pltpu.SemaphoreType.DMA((2, members)),
+            pltpu.SemaphoreType.DMA((2, tiles)),
         ],
         compiler_params=pltpu.CompilerParams(
             collective_id=0, has_side_effects=True, vmem_limit_bytes=60 * 1024 * 1024

time: 18.3 us -> 22.2 us (1.21)
  Pallas kernels: 16.1 us -> 20 us
    pallas_call x1, Pallas kernels: 16.1 us -> 20 us  [local(): pl.pallas_call(functools.partial(image_kernel, sizes), out_shape=(jax.Sha...]
where the time goes in v1:
time: 22.2 us; the launch traced here: 22 us
  Pallas kernels  20 us (90%)
  matrix products  1.98 us (9%)
    pallas_call x1, Pallas kernels, local(): pl.pallas_call(functools.partial(image_kernel, sizes), out_shape=(jax.Sha...  20 us
    dot_general x1, matrix products, local(): jnp.dot(factors, rows_out.reshape(members * 2 * pulses, lines), preferred...  1.98 us

profile of v1, /device:TPU:1, one launch (start us, length us, event | category | flops | bytes accessed | tf_op | source)
XLA Modules:
  0.0 22.0 jit_solution(16411282655226516228)
XLA Ops:
  0.0 20.0 %backproject.1 = (bf16[8,16,1024]{2,1,0:T(8,128)(2,1)}, bf16[128,128]{1,0:T(8,128)(2,1)}) custom-call(s32[2,1,8]{2,1,0:T(1,128)} %bitcast.12, s32[2,8]{1,0:T(2,128)} %bitcast.13, s32[8]{0:T(128)} %doppler_in.1, s32[8]{0:T(128)} %step_in.1, bf16[16,8192]{1,0:T(8,128)(2,1)} %bitcast.10, bf16[2,4096]{1,0:T(2,128)(2,1)} %replica_in.1, bf16[8,256,128]{2,1,0:T(8,128)(2,1)} %interp_in.1), custom_call_target="tpu_custom_call" | custom-call | tf_op jit(solution)/shard_map/backproject/pallas_call | solution.py:372
  20.1 2.0 %fusion = f32[2,64,1024]{2,1,0:T(8,128)} fusion(bf16[2,64,128]{2,1,0:T(8,128)(2,1)} %bitcast.11, bf16[128,1024,1]{1,0,2:T(8,128)(2,1)} %bitcast.9), kind=kOutput, calls=%fused_computation | convolution fusion | flops 33554432 | bytes 819200 | tf_op jit(solution)/shard_map/dot_general | solution.py:419

commit v2 on v1

--- a/solution.py
+++ b/solution.py
@@ -152,24 +152,29 @@
 
     load_replica.wait()
 
-    wide = (chirp_blocks + 1) * LANES
+    wide = chirp_blocks + 1
+    taps = replica_ref[...]
+    flip = (
+        lax.broadcasted_iota(jnp.int32, (LANES, LANES), 0)
+        + lax.broadcasted_iota(jnp.int32, (LANES, LANES), 1) == LANES - 1
+    ).astype(jnp.bfloat16)
+    by_block = jnp.concatenate([taps[:, block * LANES:(block + 1) * LANES] for block in range(chirp_blocks)], axis=0)
+    flipped = jnp.dot(by_block, flip, preferred_element_type=jnp.float32)
 
     def shifted(part):
-        taps = replica_ref[...].astype(jnp.float32)[part:part + 1, :]
-        taps = jnp.concatenate([taps, jnp.zeros((1, LANES), jnp.float32)], axis=1)
-        spread = jnp.broadcast_to(taps, (LANES, wide))
-        return pltpu.roll(spread, 0, 1, stride=1, stride_axis=0).astype(jnp.bfloat16)
-
-    shifted_re = shifted(0)
-    for turn in range(chirp_blocks + 1):
-        block = shifted_re[:, turn * LANES:(turn + 1) * LANES]
+        pieces = [flipped[2 * block + part:2 * block + part + 1] for block in reversed(range(chirp_blocks))]
+        line = jnp.concatenate([jnp.zeros((1, LANES), jnp.float32)] + pieces, axis=1)
+        spread = jnp.broadcast_to(line, (LANES, wide * LANES))
+        moved = pltpu.roll(spread, 1, 1, stride=1, stride_axis=0).astype(jnp.bfloat16)
+        places = [(wide - turn) % wide for turn in range(wide)]
+        return [moved[:, place * LANES:(place + 1) * LANES] for place in places]
+
+    for turn, block in enumerate(shifted(0)):
         chirp[turn, :LANES, :LANES] = block
         chirp[turn, LANES:, LANES:] = block
-    shifted_im = shifted(1)
-    for turn in range(chirp_blocks + 1):
-        block = shifted_im[:, turn * LANES:(turn + 1) * LANES]
-        chirp[turn, :LANES, LANES:] = block
-        chirp[turn, LANES:, :LANES] = -block
+    for turn, block in enumerate(shifted(1)):
+        chirp[turn, LANES:, :LANES] = block
+        chirp[turn, :LANES, LANES:] = -block
 
     def lay(block, values):
         ext_re[block * pulses:(block + 1) * pulses, :] = values[:pulses]
@@ -210,7 +215,7 @@
 
     rows = TILE_GROUP * pulses
     cut = band_blocks // 2 + 1
-    parts = [(0, cut), (cut, band_blocks)] if tiles == TILE_GROUP else [(0, band_blocks)]
+    parts = [(0, band_blocks)]
     spans = [
         pl.ds(max(start - 1, 0) * LANES, (stop - 1 - max(start - 1, 0)) * LANES) for start, stop in parts
     ]
@@ -231,7 +236,7 @@
         for turn in range(chirp_blocks + 1):
             total = total + lax.dot_general(
                 gat[(turn + start) * rows:(turn + stop) * rows, :], chirp[turn],
-                (((1,), (1,)), ((), ())), preferred_element_type=jnp.float32,
+                (((1,), (0,)), ((), ())), preferred_element_type=jnp.float32,
             )
         made = total.astype(jnp.bfloat16)
         bands = before + [made[j * rows:(j + 1) * rows] for j in range(stop - start)]
@@ -255,7 +260,7 @@
                 own_rows[pair * TILE_GROUP + which, :, j * LANES:(j + 1) * LANES] = steered.astype(jnp.bfloat16)
         return bands[-1:]
 
-    relay = groups == 4
+    relay = False
     relays = jnp.logical_or(group_id == 1, group_id == groups - 2)
 
     def rows_copy(part, turn, step):

time: 22.2 us -> 18.3 us (0.82)
  Pallas kernels: 20 us -> 16.2 us
    pallas_call x1, Pallas kernels: 20 us -> 16.2 us  [local(): pl.pallas_call(functools.partial(image_kernel, sizes), out_shape=(jax.Sha...]
where the time goes in v2:
time: 18.3 us; the launch traced here: 18.2 us
  Pallas kernels  16.2 us (89%)
  matrix products  1.98 us (11%)
    pallas_call x1, Pallas kernels, local(): pl.pallas_call(functools.partial(image_kernel, sizes), out_shape=(jax.Sha...  16.2 us
    dot_general x1, matrix products, local(): jnp.dot(factors, rows_out.reshape(members * 2 * pulses, lines), preferred...  1.98 us

profile of v2, /device:TPU:1, one launch (start us, length us, event | category | flops | bytes accessed | tf_op | source)
XLA Modules:
  0.0 18.2 jit_solution(9594000762757831444)
XLA Ops:
  0.0 16.2 %backproject.1 = (bf16[8,16,1024]{2,1,0:T(8,128)(2,1)}, bf16[128,128]{1,0:T(8,128)(2,1)}) custom-call(s32[2,1,8]{2,1,0:T(1,128)} %bitcast.12, s32[2,8]{1,0:T(2,128)} %bitcast.13, s32[8]{0:T(128)} %doppler_in.1, s32[8]{0:T(128)} %step_in.1, bf16[16,8192]{1,0:T(8,128)(2,1)} %bitcast.10, bf16[2,4096]{1,0:T(2,128)(2,1)} %replica_in.1, bf16[8,256,128]{2,1,0:T(8,128)(2,1)} %interp_in.1), custom_call_target="tpu_custom_call" | custom-call | tf_op jit(solution)/shard_map/backproject/pallas_call | solution.py:377
  16.2 2.0 %fusion = f32[2,64,1024]{2,1,0:T(8,128)} fusion(bf16[2,64,128]{2,1,0:T(8,128)(2,1)} %bitcast.11, bf16[128,1024,1]{1,0,2:T(8,128)(2,1)} %bitcast.9), kind=kOutput, calls=%fused_computation | convolution fusion | flops 33554432 | bytes 819200 | tf_op jit(solution)/shard_map/dot_general | solution.py:424

commit v3 on v2

--- a/solution.py
+++ b/solution.py
@@ -260,7 +260,7 @@
                 own_rows[pair * TILE_GROUP + which, :, j * LANES:(j + 1) * LANES] = steered.astype(jnp.bfloat16)
         return bands[-1:]
 
-    relay = False
+    relay = groups == 4
     relays = jnp.logical_or(group_id == 1, group_id == groups - 2)
 
     def rows_copy(part, turn, step):
@@ -354,6 +354,31 @@
         def _():
             for part in range(len(parts)):
                 each(tiles, lambda step: relay_copy(part, step).wait_send())
+
+
+def sum_kernel(factor_in, rows_in, out_ref, factor, rows, image, load_sem, store_sem):
+    pieces = load_sem.shape[0] - 1
+    width = rows.shape[1] // pieces
+    load_factor = pltpu.make_async_copy(factor_in, factor, load_sem.at[pieces])
+    load_factor.start()
+    spans = [pl.ds(piece * width, width) for piece in range(pieces)]
+    loads = [
+        pltpu.make_async_copy(rows_in.at[:, span], rows.at[:, span], load_sem.at[piece])
+        for piece, span in enumerate(spans)
+    ]
+    stores = [
+        pltpu.make_async_copy(image.at[:, span], out_ref.at[:, span], store_sem.at[piece])
+        for piece, span in enumerate(spans)
+    ]
+    for load in loads:
+        load.start()
+    load_factor.wait()
+    for span, load, store in zip(spans, loads, stores):
+        load.wait()
+        image[:, span] = jnp.dot(factor[...], rows[:, span], preferred_element_type=jnp.float32)
+        store.start()
+    for store in stores:
+        store.wait()
 
 
 def local(echo, replica, interp, band_start, visible, doppler, range_step):
@@ -421,9 +446,23 @@
         band_start.transpose(1, 2, 0), visible.T, doppler, range_step,
         echo.reshape(2 * pulses, samples), replica, interp,
     )
-    image = jnp.dot(
-        factors, rows_out.reshape(members * 2 * pulses, lines), preferred_element_type=jnp.float32
-    )
+    depth = members * 2 * pulses
+    pieces = 4
+    image = pl.pallas_call(
+        sum_kernel,
+        out_shape=jax.ShapeDtypeStruct((2 * AZ_DEV, lines), jnp.float32),
+        in_specs=[hbm] * 2,
+        out_specs=hbm,
+        scratch_shapes=[
+            pltpu.VMEM((2 * AZ_DEV, depth), jnp.bfloat16),
+            pltpu.VMEM((depth, lines), jnp.bfloat16),
+            pltpu.VMEM((2 * AZ_DEV, lines), jnp.float32),
+            pltpu.SemaphoreType.DMA((pieces + 1,)),
+            pltpu.SemaphoreType.DMA((pieces,)),
+        ],
+        compiler_params=pltpu.CompilerParams(vmem_limit_bytes=60 * 1024 * 1024),
+        name="sum_pulses",
+    )(factors, rows_out.reshape(depth, lines))
     return image.reshape(2, AZ_DEV, lines)
 
 

time: 18.3 us -> 19.3 us (1.055)
  Pallas kernels: 16.2 us -> 19.1 us
  matrix products: 1.98 us -> 0 us
    pallas_call x0 -> x1, Pallas kernels: none -> 2.26 us  [local(): pl.pallas_call(sum_kernel, out_shape=jax.ShapeDtypeStruct((2 * AZ_DEV, li...]
    dot_general x1 -> x0, matrix products: 1.98 us -> none  [local(): jnp.dot(factors, rows_out.reshape(members * 2 * pulses, lines), preferred...]
    pallas_call x1, Pallas kernels: 16.2 us -> 16.8 us  [local(): pl.pallas_call(functools.partial(image_kernel, sizes), out_shape=(jax.Sha...]
where the time goes in v3:
time: 19.3 us; the launch traced here: 19.1 us
  Pallas kernels  19.1 us (99%)
    pallas_call x1, Pallas kernels, local(): pl.pallas_call(functools.partial(image_kernel, sizes), out_shape=(jax.Sha...  16.8 us
    pallas_call x1, Pallas kernels, local(): pl.pallas_call(sum_kernel, out_shape=jax.ShapeDtypeStruct((2 * AZ_DEV, li...  2.26 us

profile of v3, /device:TPU:1, one launch (start us, length us, event | category | flops | bytes accessed | tf_op | source)
XLA Modules:
  0.0 19.1 jit_solution(7702674005809490254)
XLA Ops:
  0.0 16.8 %backproject.1 = (bf16[8,16,1024]{2,1,0:T(8,128)(2,1)}, bf16[128,128]{1,0:T(8,128)(2,1)}) custom-call(s32[2,1,8]{2,1,0:T(1,128)} %bitcast.7, s32[2,8]{1,0:T(2,128)} %bitcast.8, s32[8]{0:T(128)} %doppler_in.1, s32[8]{0:T(128)} %step_in.1, bf16[16,8192]{1,0:T(8,128)(2,1)} %bitcast.6, bf16[2,4096]{1,0:T(2,128)(2,1)} %replica_in.1, bf16[8,256,128]{2,1,0:T(8,128)(2,1)} %interp_in.1), custom_call_target="tpu_custom_call" | custom-call | tf_op jit(solution)/shard_map/backproject/pallas_call | solution.py:402
  16.9 2.3 %sum_pulses.1 = f32[128,1024]{1,0:T(8,128)} custom-call(bf16[128,128]{1,0:T(8,128)(2,1)} %get-tuple-element.7.factor_in, bf16[128,1024]{1,0:T(8,128)(2,1)} %bitcast.5), custom_call_target="tpu_custom_call" | custom-call | tf_op jit(solution)/shard_map/sum_pulses/pallas_call | solution.py:451

commit v4 on v2

--- a/solution.py
+++ b/solution.py
@@ -232,12 +232,11 @@
         gat[:, LANES:] = gat_im[...].astype(jnp.bfloat16)
 
     def steer(pair, start, stop, before):
-        total = jnp.zeros(((stop - start) * rows, 2 * LANES), jnp.float32)
-        for turn in range(chirp_blocks + 1):
-            total = total + lax.dot_general(
-                gat[(turn + start) * rows:(turn + stop) * rows, :], chirp[turn],
-                (((1,), (0,)), ((), ())), preferred_element_type=jnp.float32,
-            )
+        seen = jnp.concatenate(
+            [gat[(turn + start) * rows:(turn + stop) * rows, :] for turn in range(chirp_blocks + 1)], axis=1
+        )
+        matrix = chirp[...].reshape((chirp_blocks + 1) * 2 * LANES, 2 * LANES)
+        total = jnp.dot(seen, matrix, preferred_element_type=jnp.float32)
         made = total.astype(jnp.bfloat16)
         bands = before + [made[j * rows:(j + 1) * rows] for j in range(stop - start)]
         for here, after, j in zip(bands, bands[1:], range(start - len(before), stop - 1)):

time: 18.3 us -> 18.3 us (level)
  no operation moved by 1% of the time
where the time goes in v4:
time: 18.3 us; the launch traced here: 18.2 us
  Pallas kernels  16.2 us (89%)
  matrix products  1.98 us (11%)
    pallas_call x1, Pallas kernels, local(): pl.pallas_call(functools.partial(image_kernel, sizes), out_shape=(jax.Sha...  16.2 us
    dot_general x1, matrix products, local(): jnp.dot(factors, rows_out.reshape(members * 2 * pulses, lines), preferred...  1.98 us

profile of v4, /device:TPU:1, one launch (start us, length us, event | category | flops | bytes accessed | tf_op | source)
XLA Modules:
  0.0 18.2 jit_solution(10115340415558533655)
XLA Ops:
  0.0 16.2 %backproject.1 = (bf16[8,16,1024]{2,1,0:T(8,128)(2,1)}, bf16[128,128]{1,0:T(8,128)(2,1)}) custom-call(s32[2,1,8]{2,1,0:T(1,128)} %bitcast.12, s32[2,8]{1,0:T(2,128)} %bitcast.13, s32[8]{0:T(128)} %doppler_in.1, s32[8]{0:T(128)} %step_in.1, bf16[16,8192]{1,0:T(8,128)(2,1)} %bitcast.10, bf16[2,4096]{1,0:T(2,128)(2,1)} %replica_in.1, bf16[8,256,128]{2,1,0:T(8,128)(2,1)} %interp_in.1), custom_call_target="tpu_custom_call" | custom-call | tf_op jit(solution)/shard_map/backproject/pallas_call | solution.py:376
  16.2 2.0 %fusion = f32[2,64,1024]{2,1,0:T(8,128)} fusion(bf16[2,64,128]{2,1,0:T(8,128)(2,1)} %bitcast.11, bf16[128,1024,1]{1,0,2:T(8,128)(2,1)} %bitcast.9), kind=kOutput, calls=%fused_computation | convolution fusion | flops 33554432 | bytes 819200 | tf_op jit(solution)/shard_map/dot_general | solution.py:423
